TPU v7x, 128 devices: a whole 4x4x4 slice. The times are simulated.
128 devices in a mesh: row: 8 (over y, core), col: 16 (over x, z).
Axes of the slice: x: 4, y: 4, z: 4, core: 2. Of those that a mesh axis runs over, the one named last changes fastest.
Arguments:
- tokens: bfloat16 [512, 8192], P('row', 'col'), may hold values from -6 to 6
- w_gate: bfloat16 [8192, 28672], P('col', 'row'), may hold values from -0.0625 to 0.0625
- w_up: bfloat16 [8192, 28672], P('col', 'row'), may hold values from -0.0625 to 0.0625
- w_down: bfloat16 [28672, 8192], P('row', 'col'), may hold values from -0.03125 to 0.03125
- cotangent: bfloat16 [512, 8192], P('row', 'col'), may hold values from -1.1953125 to 1.1953125
Outputs:
- mixed: bfloat16 [512, 8192], P('row', 'col')
- input_grad: bfloat16 [512, 8192], P('row', 'col')
- gate_wgrad: bfloat16 [8192, 28672], P('col', 'row')
- up_wgrad: bfloat16 [8192, 28672], P('col', 'row')
- down_wgrad: bfloat16 [28672, 8192], P('row', 'col')
All inputs are finite; a program needn't handle non-finite values.
Results may differ from a plain program's by a relative error of at most 0.005.
Values may be sent and summed in bfloat16 or wider, within the bound.
A program may use at most 128 MiB of HBM per device.

v0:
```python
import jax
import jax.numpy as jnp
from jax import lax
from jax.sharding import PartitionSpec as P


def matmul_nt(left, right):
    return lax.dot_general(
        left, right, (((1,), (1,)), ((), ())), preferred_element_type=jnp.float32
    )


def matmul_tn(left, right):
    return lax.dot_general(
        left, right, (((0,), (0,)), ((), ())), preferred_element_type=jnp.float32
    )


def shards(tokens, w_gate, w_up, w_down, cotangent):
    hidden_width = w_gate.shape[1]
    gathered = lax.all_gather(tokens, "row", axis=0, tiled=True)
    block_rows = gathered
    gate_and_up = lax.psum_scatter(
        jnp.concatenate(
            [
                jnp.dot(block_rows, w_gate, preferred_element_type=jnp.float32),
                jnp.dot(block_rows, w_up, preferred_element_type=jnp.float32),
            ],
            axis=1,
        ),
        "col",
        scatter_dimension=0,
        tiled=True,
    )
    gate = gate_and_up[:, :hidden_width]
    up = gate_and_up[:, hidden_width:]
    activated = jax.nn.silu(gate)
    hidden = (activated * up).astype(jnp.bfloat16)
    hidden_all = lax.all_gather(hidden, "col", axis=0, tiled=True)
    block_rows = hidden_all
    mixed = lax.psum_scatter(
        jnp.dot(block_rows, w_down, preferred_element_type=jnp.float32),
        "row",
        scatter_dimension=0,
        tiled=True,
    ).astype(jnp.bfloat16)
    cotan_all = lax.all_gather(cotangent, "row", axis=0, tiled=True)
    block_rows = cotan_all
    hidden_grad = lax.psum_scatter(
        matmul_nt(block_rows, w_down), "col", scatter_dimension=0, tiled=True
    )
    sigmoid_gate = jax.nn.sigmoid(gate)
    gate_grad = (hidden_grad * up * sigmoid_gate * (1.0 + gate * (1.0 - sigmoid_gate))).astype(
        jnp.bfloat16
    )
    up_grad = (hidden_grad * activated).astype(jnp.bfloat16)
    gate_grad_all, up_grad_all = (
        lax.all_gather(gate_grad, "col", axis=0, tiled=True),
        lax.all_gather(up_grad, "col", axis=0, tiled=True),
    )
    down_wgrad = matmul_tn(hidden_all, cotan_all).astype(jnp.bfloat16)
    gate_wgrad = matmul_tn(gathered, gate_grad_all).astype(jnp.bfloat16)
    up_wgrad = matmul_tn(gathered, up_grad_all).astype(jnp.bfloat16)
    input_grad = lax.psum_scatter(
        matmul_nt(gate_grad_all, w_gate) + matmul_nt(up_grad_all, w_up),
        "row",
        scatter_dimension=0,
        tiled=True,
    ).astype(jnp.bfloat16)
    return (mixed, input_grad, gate_wgrad, up_wgrad, down_wgrad)


def solution(mesh):
    return jax.shard_map(
        shards,
        mesh=mesh,
        in_specs=(
            P("row", "col"),
            P("col", "row"),
            P("col", "row"),
            P("row", "col"),
            P("row", "col"),
        ),
        out_specs=(
            P("row", "col"),
            P("row", "col"),
            P("col", "row"),
            P("col", "row"),
            P("row", "col"),
        ),
        check_vma=False,
    )
```

profile of v0, /device:TPU:1, one launch (start us, length us, event | category | flops | bytes accessed | tf_op | source)
XLA Modules:
  0.0 445.7 jit_solution(16200010160371691720)
XLA Ops:
  7.2 15.2 %all_gather.17 = bf16[512,512]{1,0:T(8,128)(2,1)S(1)} all-gather(bf16[64,512]{1,0:T(8,128)(2,1)} %param.9), channel_id=1, replica_groups=mesh['row'=8,'col'=16] {'row'}, dimensions={0}, use_global_device_ids=true | all-gather | bytes 589824 | tf_op jit(solution)/shard_map/all_gather | solution.py:47
  22.4 7.1 %fusion.6 = f32[512,3584]{1,0:T(8,128)} fusion(bf16[512,512]{1,0:T(8,128)(2,1)S(1)} %all_gather.17, bf16[3584,512]{1,0:T(8,128)(2,1)} %param.8), kind=kOutput, calls=%fused_computation.15 | convolution fusion | flops 1879048192 | bytes 11534336 | tf_op jit(solution)/shard_map/dot_general | solution.py:8
  29.5 0.8 copy-done.1
  30.3 13.1 %all_gather.15 = bf16[512,512]{1,0:T(8,128)(2,1)S(1)} all-gather(bf16[64,512]{1,0:T(8,128)(2,1)S(1)} %copy-done.1), channel_id=1, replica_groups=mesh['row'=8,'col'=16] {'row'}, dimensions={0}, use_global_device_ids=true | all-gather | bytes 589824 | tf_op jit(solution)/shard_map/all_gather | solution.py:21
  43.4 4.3 fusion.3
  47.7 2.1 fusion.4
  49.8 5.6 %pad_maximum_fusion = f32[512,7168]{1,0:T(8,128)} fusion(f32[512,3584]{1,0:T(8,128)S(1)} %fusion.4, f32[512,3584]{1,0:T(8,128)S(1)} %fusion.3), kind=kLoop, calls=%fused_computation | loop fusion | flops 3670016 | bytes 29360128 | tf_op jit(solution)/shard_map/concatenate | solution.py:24
  55.4 57.2 %reduce-scatter.9.cloned.1.call-done = f32[32,3584]{1,0:T(8,128)} async-done(((f32[512,3584]{1,0:T(8,128)}), f32[32,3584]{1,0:T(8,128)}) %reduce-scatter.9.cloned.1.call-update) | async-done | bytes 458768 | tf_op jit(solution)/shard_map/reduce_scatter | solution.py:49
  112.7 105.4 %reduce-scatter.5.cloned.1.call-done = f32[32,7168]{1,0:T(8,128)} async-done(((f32[512,7168]{1,0:T(8,128)}), f32[32,7168]{1,0:T(8,128)}) %reduce-scatter.5.cloned.1.call-update) | async-done | bytes 917520 | tf_op jit(solution)/shard_map/reduce_scatter | solution.py:23
  218.1 2.3 multiply_convert_fusion
  221.7 47.9 %all-gather.6.cloned.1.call-done = bf16[512,3584]{1,0:T(8,128)(2,1)} async-done(((bf16[32,3584]{1,0:T(8,128)(2,1)}), bf16[512,3584]{1,0:T(8,128)(2,1)}) %all-gather.6.cloned.1.call-update) | async-done | bytes 3670032 | tf_op jit(solution)/shard_map/all_gather | solution.py:58
  269.6 5.2 %fusion.7 = f32[512,512]{1,0:T(8,128)S(1)} fusion(bf16[512,3584]{1,0:T(8,128)(2,1)} %all-gather.6.cloned.1.call-done, bf16[512,3584]{1,0:T(8,128)(2,1)} %param.6), kind=kOutput, calls=%fused_computation.16 | convolution fusion | flops 1879048192 | bytes 8388608 | tf_op jit(solution)/shard_map/dot_general | solution.py:8
  274.8 46.5 %all-gather.8.cloned.1.call-done = bf16[512,3584]{1,0:T(8,128)(2,1)} async-done(((bf16[32,3584]{1,0:T(8,128)(2,1)}), bf16[512,3584]{1,0:T(8,128)(2,1)}) %all-gather.8.cloned.1.call-update) | async-done | bytes 3670032 | tf_op jit(solution)/shard_map/all_gather | solution.py:59
  321.4 6.3 %convolution_add_fusion = f32[512,512]{1,0:T(8,128)} fusion(f32[512,512]{1,0:T(8,128)S(1)} %fusion.7, bf16[512,3584]{1,0:T(8,128)(2,1)} %all-gather.8.cloned.1.call-done, bf16[512,3584]{1,0:T(8,128)(2,1)} %param.7), kind=kOutput, calls=%fused_computation.6 | convolution fusion | flops 1879310336 | bytes 9437184 | tf_op jit(solution)/shard_map/dot_general | solution.py:8
  327.9 45.2 %all-gather.4.cloned.1.call-done = bf16[512,3584]{1,0:T(8,128)(2,1)} async-done(((bf16[32,3584]{1,0:T(8,128)(2,1)}), bf16[512,3584]{1,0:T(8,128)(2,1)}) %all-gather.4.cloned.1.call-update) | async-done | bytes 3670032 | tf_op jit(solution)/shard_map/all_gather | solution.py:39
  373.1 6.2 %fusion.5 = f32[512,512]{1,0:T(8,128)} fusion(bf16[512,3584]{1,0:T(8,128)(2,1)} %all-gather.4.cloned.1.call-done, bf16[3584,512]{1,0:T(8,128)(2,1)} %param.8), kind=kOutput, calls=%fused_computation.14 | convolution fusion | flops 1879048192 | bytes 8388608 | tf_op jit(solution)/shard_map/dot_general | solution.py:42
  379.3 6.0 %fusion = bf16[512,3584]{0,1:T(8,128)(2,1)} fusion(bf16[512,3584]{1,0:T(8,128)(2,1)} %all-gather.6.cloned.1.call-done, bf16[512,512]{1,0:T(8,128)(2,1)S(1)} %all_gather.15), kind=kOutput, calls=%fused_computation.4 | convolution fusion | flops 1880883200 | bytes 7864320 | tf_op jit(solution)/shard_map/dot_general | solution.py:14
  385.3 5.9 %copy.10 = bf16[512,3584]{1,0:T(8,128)(2,1)} copy(bf16[512,3584]{0,1:T(8,128)(2,1)} %fusion) | data formatting | bytes 7340032
  391.3 6.0 %fusion.1 = bf16[512,3584]{0,1:T(8,128)(2,1)} fusion(bf16[512,3584]{1,0:T(8,128)(2,1)} %all-gather.8.cloned.1.call-done, bf16[512,512]{1,0:T(8,128)(2,1)S(1)} %all_gather.15), kind=kOutput, calls=%fused_computation.5 | convolution fusion | flops 1880883200 | bytes 7864320 | tf_op jit(solution)/shard_map/dot_general | solution.py:14
  397.3 5.9 %copy.11 = bf16[512,3584]{1,0:T(8,128)(2,1)} copy(bf16[512,3584]{0,1:T(8,128)(2,1)} %fusion.1) | data formatting | bytes 7340032
  403.2 6.0 %convolution_convert_fusion = bf16[3584,512]{1,0:T(8,128)(2,1)} fusion(bf16[512,3584]{1,0:T(8,128)(2,1)} %all-gather.4.cloned.1.call-done, bf16[512,512]{1,0:T(8,128)(2,1)S(1)} %all_gather.17), kind=kOutput, calls=%fused_computation.1 | convolution fusion | flops 1880883200 | bytes 7864320 | tf_op jit(solution)/shard_map/dot_general | solution.py:14
  409.2 1.5 convert_element_type.34
  410.8 26.6 %reduce-scatter.7.cloned.1.call-done = f32[64,512]{1,0:T(8,128)} async-done(((f32[512,512]{1,0:T(8,128)}), f32[64,512]{1,0:T(8,128)}) %reduce-scatter.7.cloned.1.call-update) | async-done | bytes 131088 | tf_op jit(solution)/shard_map/reduce_scatter | solution.py:41
  437.3 1.5 convert_element_type.31
  (18 shorter events, 1.6 us)
Async XLA Ops:
  7.2 105.5 %reduce-scatter.9.cloned.1.call-start = ((), (), s32[]{:S(2)}) async-start(), calls=%async_computation.7 | async-start | bytes 7798784 | tf_op jit(solution)/shard_map/reduce_scatter | solution.py:49
  29.5 0.8 copy-start.1
  29.5 188.6 %reduce-scatter.5.cloned.1.call-start = ((), (), s32[]{:S(2)}) async-start(), calls=%async_computation.4 | async-start | bytes 15597568 | tf_op jit(solution)/shard_map/reduce_scatter | solution.py:23
  43.4 4.3 copy-start
  55.4 214.2 %all-gather.6.cloned.1.call-start = ((), (), s32[]{:S(2)}) async-start(), calls=%async_computation.8 | async-start | bytes 3899392 | tf_op jit(solution)/shard_map/all_gather | solution.py:58
  220.5 100.9 %all-gather.8.cloned.1.call-start = ((), (), s32[]{:S(2)}) async-start(), calls=%async_computation.9 | async-start | bytes 3899392 | tf_op jit(solution)/shard_map/all_gather | solution.py:59
  221.0 152.1 %all-gather.4.cloned.1.call-start = ((), (), s32[]{:S(2)}) async-start(), calls=%async_computation.5 | async-start | bytes 3899392 | tf_op jit(solution)/shard_map/all_gather | solution.py:39
  221.6 187.6 %reduce-scatter.11.cloned.1.call-start = ((), (), s32[]{:S(2)}) async-start(), calls=%async_computation.10 | async-start | bytes 1179648 | tf_op jit(solution)/shard_map/reduce_scatter | solution.py:64
  327.7 109.7 %reduce-scatter.7.cloned.1.call-start = ((), (), s32[]{:S(2)}) async-start(), calls=%async_computation.6 | async-start | bytes 1179648 | tf_op jit(solution)/shard_map/reduce_scatter | solution.py:41
Sparse Core Ops, SparseCore 0:
  29.6 83.0 reduce-scatter.8
  116.5 101.5 reduce-scatter.4
  221.1 48.4 all-gather.5
  272.5 48.8 all-gather.7
  324.2 48.8 all-gather.3
  375.5 28.5 reduce-scatter.10
  406.6 30.6 reduce-scatter.6
where the time goes:
time: 448 us; the launch traced here: 446 us
  waiting for transfers between devices  330 us (74%)
  matrix products  49.1 us (11%)
  blocking collectives  28.3 us (6%)
  between operations  14.2 us (3%)
  local copies, waits for them, and re-layouts  12.6 us (3%)
  other arithmetic  11 us (2%)
    reduce_scatter x1, waiting for transfers between devices, shards(): lax.psum_scatter(jnp.concatenate([jnp.dot(block_rows, w_gate, preferred_e...  105 us
    reduce_scatter x1, waiting for transfers between devices, shards(): lax.psum_scatter(matmul_nt(block_rows, w_down), 'col', scatter_dimension=...  57.2 us
    all_gather x1, waiting for transfers between devices, shards(): lax.all_gather(gate_grad, 'col', axis=0, tiled=True)  47.9 us
    all_gather x1, waiting for transfers between devices, shards(): lax.all_gather(up_grad, 'col', axis=0, tiled=True)  46.5 us
    all_gather x1, waiting for transfers between devices, shards(): hidden_all = lax.all_gather(hidden, 'col', axis=0, tiled=True)  45.2 us
    reduce_scatter x1, waiting for transfers between devices, shards(): lax.psum_scatter(jnp.dot(block_rows, w_down, preferred_element_type=jnp.f...  26.6 us
    dot_general x3, matrix products, matmul_nt(): lax.dot_general(left, right, (((1,), (1,)), ((), ())), preferred_element_...  18.6 us
    dot_general x3, matrix products, matmul_tn(): lax.dot_general(left, right, (((0,), (0,)), ((), ())), preferred_element_...  18 us
  transfers between devices with their start and end apart: 7, of which 6 were waited for; matrix products, arithmetic and copies ran while one was open for 14% of the time, Pallas kernels for 0%

commit v1 on v0

v1 whole, which is shorter than its diff:
```python
import jax
import jax.numpy as jnp
from jax import lax
from jax.experimental import pallas as pl
from jax.experimental.pallas import tpu as pltpu
from jax.sharding import PartitionSpec as P

MESH = pl.DeviceIdType.MESH
BF16 = jnp.bfloat16
F32 = jnp.float32
WIDTH = 256
DEPTH = 8

FAR_UP, FAR_DOWN, OWN_UP, OWN_DOWN, SUM_UP, SUM_DOWN = range(6)
SECOND = 6
GIVE_UP, GIVE_DOWN, PASS_UP, PASS_DOWN = range(12, 16)
WIDE_UP, WIDE_DOWN, WIDE_PASS_UP, WIDE_PASS_DOWN = range(16, 20)
COPIES = 20


def dot(left, right):
    return jnp.dot(left, right, preferred_element_type=F32)


def dot_nt(left, right):
    return lax.dot_general(left, right, (((1,), (1,)), ((), ())), preferred_element_type=F32)


def ring_kernel(
    steps,
    tok_ref, cot_ref, wg_hbm, wu_hbm, wd_hbm,
    hid_out, gg_out, ug_out, tok_out, cot_out, mi_out,
    wg, wu, wd, nat, perm, far, far_in, near, near_in,
    far2, far2_in, near2, near2_in, sub, all3, acc, core_in, y_send, y_in,
    send_sem, recv_sem, w_sem, out_sem, g_send, g_recv, r_send, r_recv, tok_sem,
):
    row, col = lax.axis_index("row"), lax.axis_index("col")
    x, z, y, core = col // 4, col % 4, row // 2, row % 2
    width = WIDTH

    def at_x(i):
        return (row, lax.rem(i, 4) * 4 + z)

    def at_z(i):
        return (row, x * 4 + lax.rem(i, 4))

    def at_y(i):
        return (lax.rem(i, 4) * 2 + core, col)

    sibling = (row + 1 - 2 * core, col)
    rings = ((x, z, at_x, at_z), (z, x, at_z, at_x))

    for k in range(steps):
        cols = pl.ds(k * 2 * width, 2 * width)
        pltpu.make_async_copy(wd_hbm.at[cols, :], wd.at[k], w_sem.at[k, 2]).start()
        pltpu.make_async_copy(wg_hbm.at[:, cols], wg.at[k], w_sem.at[k, 0]).start()
        pltpu.make_async_copy(wu_hbm.at[:, cols], wu.at[k], w_sem.at[k, 1]).start()

    for half in range(2):
        nat[0, y, 2 * core + half] = tok_ref[32 * half : 32 * half + 32, :]
        nat[1, y, 2 * core + half] = cot_ref[32 * half : 32 * half + 32, :]

    barrier = pltpu.get_barrier_semaphore()
    peers = [at_x(x + 1), at_x(x + 3), at_z(z + 1), at_z(z + 3), at_y(y + 1), at_y(y + 2), at_y(y + 3), sibling]
    for peer in peers:
        pl.semaphore_signal(barrier, inc=1, device_id=peer, device_id_type=MESH)
    pl.semaphore_wait(barrier, len(peers))

    def rows_of(y_at, core_at):
        return nat.at[:, y_at, pl.ds(2 * core_at, 2)]

    def y_copy(step):
        return pltpu.make_async_remote_copy(
            src_ref=rows_of(y, core), dst_ref=rows_of(y, core), send_sem=g_send.at[step], recv_sem=g_recv.at[step],
            device_id=at_y(y + step), device_id_type=MESH,
        )

    def y_arrival(step):
        came = lax.rem(y + 4 - step, 4)
        return pltpu.make_async_remote_copy(
            src_ref=rows_of(came, core), dst_ref=rows_of(came, core), send_sem=g_send.at[step],
            recv_sem=g_recv.at[step], device_id=at_y(y + step), device_id_type=MESH,
        )

    def core_copy(step, core_at):
        came = lax.rem(y + 4 - step, 4)
        return pltpu.make_async_remote_copy(
            src_ref=rows_of(came, core_at), dst_ref=rows_of(came, core_at), send_sem=g_send.at[4 + step],
            recv_sem=g_recv.at[4 + step], device_id=sibling, device_id_type=MESH,
        )

    for step in (2, 1, 3):
        y_copy(step).start()
    core_copy(0, core).start()
    for step in (1, 3, 2):
        y_arrival(step).wait_recv()
        core_copy(step, core).start()
    for step in range(4):
        core_copy(step, 1 - core).wait_recv()
    for step in (1, 2, 3):
        y_copy(step).wait_send()
    for step in range(4):
        core_copy(step, core).wait_send()

    for i in range(4):
        for j in range(4):
            perm[:, j, i] = nat[:, i, j]
    keep = (
        pltpu.make_async_copy(nat.at[0], tok_out, tok_sem.at[0]),
        pltpu.make_async_copy(nat.at[1], cot_out, tok_sem.at[1]),
    )
    for copy in keep:
        copy.start()
    acc[...] = jnp.zeros_like(acc)

    def part(h, k, a, block, first, count):
        tokens = (nat, perm)[h]
        left = tokens[1 if a == 2 else 0, block, pl.ds(first, count)].reshape(count * 32, -1)
        if a == 2:
            return dot_nt(left, wd[k, h * width : (h + 1) * width, :])
        return dot(left, (wg, wu)[a][k, :, h * width : (h + 1) * width])

    def copy_of(kind, k, h, src, dst, target):
        at = 2 * k + h
        return pltpu.make_async_remote_copy(
            src_ref=src, dst_ref=dst, send_sem=send_sem.at[at, kind], recv_sem=recv_sem.at[at, kind],
            device_id=target, device_id_type=MESH,
        )

    def copies(k, h):
        at = 2 * k + h
        p, q, at_p, at_q = rings[h]
        up, down, up2, down2 = at_p(p + 1), at_p(p + 3), at_q(q + 1), at_q(q + 3)
        q_up, q_down = lax.rem(q + 1, 4), lax.rem(q + 3, 4)
        p_up, p_down = lax.rem(p + 1, 4), lax.rem(p + 3, 4)
        table = {}

        def same(kind, src, dst, target):
            table[kind] = (src, dst, target, dst)

        for base, f, fi, n, ni, u, d in (
            (0, far, far_in, near, near_in, up, down),
            (SECOND, far2, far2_in, near2, near2_in, up2, down2),
        ):
            same(base + FAR_UP, f.at[at, 0], fi.at[at, 0], u)
            same(base + FAR_DOWN, f.at[at, 1], fi.at[at, 1], d)
            same(base + SUM_UP, n.at[at, 0, 0], ni.at[at, 0, 0], u)
            same(base + OWN_UP, n.at[at, 0, 1], ni.at[at, 0, 1], u)
            same(base + OWN_DOWN, n.at[at, 1, 0], ni.at[at, 1, 0], d)
            same(base + SUM_DOWN, n.at[at, 1, 1], ni.at[at, 1, 1], d)

        def held(kind, mine, theirs, target):
            table[kind] = (mine, mine, target, theirs)

        mine = all3.at[at, :, p, q]
        held(GIVE_UP, mine, all3.at[at, :, p, q_down], up2)
        held(GIVE_DOWN, mine, all3.at[at, :, p, q_up], down2)
        opp_q, opp_p = lax.rem(q + 2, 4), lax.rem(p + 2, 4)
        low, high = pl.ds(0, 16), pl.ds(16, 16)
        held(PASS_UP, all3.at[at, :, p, q_down, low], all3.at[at, :, p, opp_q, low], up2)
        held(PASS_DOWN, all3.at[at, :, p, q_up, high], all3.at[at, :, p, opp_q, high], down2)
        held(WIDE_UP, all3.at[at, :, p], all3.at[at, :, p_down], up)
        held(WIDE_DOWN, all3.at[at, :, p], all3.at[at, :, p_up], down)
        low, high = pl.ds(0, 2), pl.ds(2, 2)
        held(WIDE_PASS_UP, all3.at[at, :, p_down, low], all3.at[at, :, opp_p, low], up)
        held(WIDE_PASS_DOWN, all3.at[at, :, p_up, high], all3.at[at, :, opp_p, high], down)
        return table

    def start(k, h, *kinds):
        table = copies(k, h)
        for kind in kinds:
            src, dst, target, _ = table[kind]
            copy_of(kind, k, h, src, dst, target).start()

    def arrive(k, h, *kinds):
        table = copies(k, h)
        for kind in kinds:
            src, _, target, here = table[kind]
            copy_of(kind, k, h, here, here, target).wait_recv()

    def sent(k, h):
        for kind, (src, dst, target, _) in copies(k, h).items():
            copy_of(kind, k, h, src, dst, target).wait_send()

    def stage0(k):
        cols = pl.ds(0, 2 * width)
        pltpu.make_async_copy(wd_hbm.at[cols, :], wd.at[k], w_sem.at[k, 2]).wait()
        pltpu.make_async_copy(wg_hbm.at[:, cols], wg.at[k], w_sem.at[k, 0]).wait()
        pltpu.make_async_copy(wu_hbm.at[:, cols], wu.at[k], w_sem.at[k, 1]).wait()
        for h in range(2):
            p = rings[h][0]
            at = 2 * k + h
            for a in range(3):
                whole = part(h, k, a, lax.rem(p + 2, 4), 0, 4).astype(BF16)
                far[at, 0, a] = whole[:64]
                far[at, 1, a] = whole[64:]
            start(k, h, FAR_UP, FAR_DOWN)
            for a in range(3):
                near[at, 0, 1, a] = part(h, k, a, lax.rem(p + 1, 4), 2, 2).astype(BF16)
                near[at, 1, 0, a] = part(h, k, a, lax.rem(p + 3, 4), 0, 2).astype(BF16)
            start(k, h, OWN_UP, OWN_DOWN)

    def stage1(k):
        for h in range(2):
            p = rings[h][0]
            at = 2 * k + h
            arrive(k, h, FAR_UP, FAR_DOWN)
            for a in range(3):
                near[at, 0, 0, a] = (
                    part(h, k, a, lax.rem(p + 1, 4), 0, 2) + far_in[at, 0, a].astype(F32)
                ).astype(BF16)
                near[at, 1, 1, a] = (
                    part(h, k, a, lax.rem(p + 3, 4), 2, 2) + far_in[at, 1, a].astype(F32)
                ).astype(BF16)
            start(k, h, SUM_UP, SUM_DOWN)

    def stage2(k):
        slot = lax.rem(k, 3)
        for h in range(2):
            p, q = rings[h][:2]
            at = 2 * k + h
            arrive(k, h, OWN_UP, OWN_DOWN, SUM_UP, SUM_DOWN)
            for a in range(3):
                for half in range(2):
                    total = (
                        part(h, k, a, p, 2 * half, 2)
                        + near_in[at, 0, half, a].astype(F32)
                        + near_in[at, 1, half, a].astype(F32)
                    )
                    sub[slot, h, a, 2 * half] = total[:32]
                    sub[slot, h, a, 2 * half + 1] = total[32:]
            for a in range(3):
                opposite = sub[slot, h, a, lax.rem(q + 2, 4)].astype(BF16)
                far2[at, 0, a] = opposite[:16]
                far2[at, 1, a] = opposite[16:]
                near2[at, 0, 1, a] = sub[slot, h, a, lax.rem(q + 1, 4), 16:, :].astype(BF16)
                near2[at, 1, 0, a] = sub[slot, h, a, lax.rem(q + 3, 4), :16, :].astype(BF16)
            start(k, h, *(SECOND + kind for kind in (FAR_UP, FAR_DOWN, OWN_UP, OWN_DOWN)))

    def stage3(k):
        slot = lax.rem(k, 3)
        for h in range(2):
            q = rings[h][1]
            at = 2 * k + h
            arrive(k, h, SECOND + FAR_UP, SECOND + FAR_DOWN)
            for a in range(3):
                near2[at, 0, 0, a] = (
                    sub[slot, h, a, lax.rem(q + 1, 4), :16, :] + far2_in[at, 0, a].astype(F32)
                ).astype(BF16)
                near2[at, 1, 1, a] = (
                    sub[slot, h, a, lax.rem(q + 3, 4), 16:, :] + far2_in[at, 1, a].astype(F32)
                ).astype(BF16)
            start(k, h, SECOND + SUM_UP, SECOND + SUM_DOWN)

    def stage4(k):
        slot = lax.rem(k, 3)
        for h in range(2):
            p, q = rings[h][:2]
            at = 2 * k + h
            arrive(k, h, *(SECOND + kind for kind in (OWN_UP, OWN_DOWN, SUM_UP, SUM_DOWN)))
            for half in range(2):
                rows = slice(16 * half, 16 * half + 16)
                gate, up, hidden_grad = (
                    sub[slot, h, a, q, rows, :]
                    + near2_in[at, 0, half, a].astype(F32)
                    + near2_in[at, 1, half, a].astype(F32)
                    for a in range(3)
                )
                sigmoid_gate = 1.0 / (1.0 + jnp.exp(-gate))
                activated = gate * sigmoid_gate
                all3[at, 0, p, q, rows, :] = (activated * up).astype(BF16)
                all3[at, 1, p, q, rows, :] = (
                    hidden_grad * up * sigmoid_gate * (1.0 + gate * (1.0 - sigmoid_gate))
                ).astype(BF16)
                all3[at, 2, p, q, rows, :] = (hidden_grad * activated).astype(BF16)
            start(k, h, GIVE_UP, GIVE_DOWN)

    def stage5(k):
        for h in range(2):
            arrive(k, h, GIVE_UP, GIVE_DOWN)
            start(k, h, PASS_UP, PASS_DOWN)

    def stage6(k):
        for h in range(2):
            arrive(k, h, PASS_UP, PASS_DOWN)
            start(k, h, WIDE_UP, WIDE_DOWN)

    def stage7(k):
        for h in range(2):
            arrive(k, h, WIDE_UP, WIDE_DOWN)
            start(k, h, WIDE_PASS_UP, WIDE_PASS_DOWN)

    def keeps(k):
        copies_out = []
        for h in range(2):
            at = 2 * k + h
            cols = pl.ds(pl.multiple_of(at * width, width), width)
            for a, out in enumerate((hid_out, gg_out, ug_out)):
                if h == 0:
                    copies_out.append((all3.at[at, a], out.at[:, :, :, cols], 5 * a))
                else:
                    for j in range(4):
                        copies_out.append((all3.at[at, a, j], out.at[:, j, :, cols], 5 * a + 1 + j))
        return [pltpu.make_async_copy(src, dst, out_sem.at[k, n]) for src, dst, n in copies_out]

    def stage8(k):
        for h in range(2):
            arrive(k, h, WIDE_PASS_UP, WIDE_PASS_DOWN)
        for copy in keeps(k):
            copy.start()
        for h in range(2):
            at = 2 * k + h
            sent(k, h)
            hidden_rows = slice(h * width, (h + 1) * width)
            for b in range(4):
                hidden, gate_grad, up_grad = (all3[at, a, b].reshape(128, width) for a in range(3))
                mixed = dot(hidden, wd[k, hidden_rows, :])
                into = dot_nt(gate_grad, wg[k, :, hidden_rows]) + dot_nt(up_grad, wu[k, :, hidden_rows])
                for j in range(4):
                    rows = slice(32 * j, 32 * j + 32)
                    i, jj = (b, j) if h == 0 else (j, b)
                    acc[0, i, jj] += mixed[rows]
                    acc[1, i, jj] += into[rows]

    stages = (stage0, stage1, stage2, stage3, stage4, stage5, stage6, stage7, stage8)

    def turn(i, carry):
        for late, stage in enumerate(stages):
            @pl.when((i >= late) & (i < steps + late))
            def _():
                stage(i - late)
        return carry

    lax.fori_loop(0, steps + DEPTH, turn, 0)

    def acc_rows(y_at, core_at):
        return acc.at[:, y_at, pl.ds(2 * core_at, 2)]

    def core_sum(step):
        return pltpu.make_async_remote_copy(
            src_ref=acc_rows(lax.rem(y + step, 4), 1 - core), dst_ref=core_in.at[step], send_sem=r_send.at[step],
            recv_sem=r_recv.at[step], device_id=sibling, device_id_type=MESH,
        )

    def y_sum(step):
        return pltpu.make_async_remote_copy(
            src_ref=y_send.at[step], dst_ref=y_in.at[step], send_sem=r_send.at[4 + step],
            recv_sem=r_recv.at[4 + step], device_id=at_y(y + step), device_id_type=MESH,
        )

    order = (2, 1, 3, 0)
    for step in order:
        core_sum(step).start()
    for step in order:
        core_sum(step).wait_recv()
        total = acc[:, lax.rem(y + step, 4), pl.ds(2 * core, 2)] + core_in[step]
        y_send[step] = total
        if step:
            y_sum(step).start()
    for step in (1, 3, 2):
        y_sum(step).wait_recv()
    result = y_send[0] + y_in[1] + y_in[2] + y_in[3]
    for j in range(2):
        mi_out[:, 32 * j : 32 * j + 32, :] = result[:, j].astype(BF16)
    for step in order:
        core_sum(step).wait_send()
        if step:
            y_sum(step).wait_send()

    for copy in keep:
        copy.wait()

    def finish(k, carry):
        for copy in keeps(k):
            copy.wait()
        return carry

    lax.fori_loop(0, steps, finish, 0)


def ring_call(tokens, w_gate, w_up, w_down, cotangent):
    features, hidden = w_gate.shape
    steps = hidden // (2 * WIDTH)
    parts = 2 * steps
    any_space = pl.BlockSpec(memory_space=pl.ANY)
    vmem = pl.BlockSpec(memory_space=pltpu.VMEM)

    def kernel(*refs):
        ring_kernel(steps, *refs)

    wide = jax.ShapeDtypeStruct((4, 4, 32, hidden), BF16)
    model = jax.ShapeDtypeStruct((4, 4, 32, features), BF16)
    dma = pltpu.SemaphoreType.DMA
    return pl.pallas_call(
        kernel,
        out_shape=(wide, wide, wide, model, model, jax.ShapeDtypeStruct((2, 64, features), BF16)),
        in_specs=[vmem, vmem, any_space, any_space, any_space],
        out_specs=(any_space,) * 5 + (vmem,),
        scratch_shapes=[
            pltpu.VMEM((steps, features, 2 * WIDTH), BF16),
            pltpu.VMEM((steps, features, 2 * WIDTH), BF16),
            pltpu.VMEM((steps, 2 * WIDTH, features), BF16),
            pltpu.VMEM((2, 4, 4, 32, features), BF16),
            pltpu.VMEM((2, 4, 4, 32, features), BF16),
            pltpu.VMEM((parts, 2, 3, 64, WIDTH), BF16),
            pltpu.VMEM((parts, 2, 3, 64, WIDTH), BF16),
            pltpu.VMEM((parts, 2, 2, 3, 64, WIDTH), BF16),
            pltpu.VMEM((parts, 2, 2, 3, 64, WIDTH), BF16),
            pltpu.VMEM((parts, 2, 3, 16, WIDTH), BF16),
            pltpu.VMEM((parts, 2, 3, 16, WIDTH), BF16),
            pltpu.VMEM((parts, 2, 2, 3, 16, WIDTH), BF16),
            pltpu.VMEM((parts, 2, 2, 3, 16, WIDTH), BF16),
            pltpu.VMEM((3, 2, 3, 4, 32, WIDTH), F32),
            pltpu.VMEM((parts, 3, 4, 4, 32, WIDTH), BF16),
            pltpu.VMEM((2, 4, 4, 32, features), F32),
            pltpu.VMEM((4, 2, 2, 32, features), F32),
            pltpu.VMEM((4, 2, 2, 32, features), F32),
            pltpu.VMEM((4, 2, 2, 32, features), F32),
            dma((parts, COPIES)),
            dma((parts, COPIES)),
            dma((steps, 3)),
            dma((steps, 15)),
            dma((8,)),
            dma((8,)),
            dma((8,)),
            dma((8,)),
            dma((2,)),
        ],
        name="ring_sums",
        compiler_params=pltpu.CompilerParams(
            collective_id=0, has_side_effects=True, vmem_limit_bytes=62 * 2**20
        ),
    )(tokens, cotangent, w_gate, w_up, w_down)


def matmul_tn(left, right):
    return lax.dot_general(left, right, (((0,), (0,)), ((), ())), preferred_element_type=F32).astype(BF16)


def shards(tokens, w_gate, w_up, w_down, cotangent):
    hidden, gate_grad, up_grad, tok_all, cot_all, sums = ring_call(tokens, w_gate, w_up, w_down, cotangent)
    hidden, gate_grad, up_grad, tok_all, cot_all = (
        a.reshape(512, a.shape[-1]) for a in (hidden, gate_grad, up_grad, tok_all, cot_all)
    )
    return (
        sums[0],
        sums[1],
        matmul_tn(tok_all, gate_grad),
        matmul_tn(tok_all, up_grad),
        matmul_tn(hidden, cot_all),
    )


def solution(mesh):
    return jax.shard_map(
        shards,
        mesh=mesh,
        in_specs=(P("row", "col"), P("col", "row"), P("col", "row"), P("row", "col"), P("row", "col")),
        out_specs=(P("row", "col"), P("row", "col"), P("col", "row"), P("col", "row"), P("row", "col")),
        check_vma=False,
    )
```

time: 448 us -> 173 us (0.39)
  waiting for transfers between devices: 330 us -> 0 us
  Pallas kernels: 0 us -> 156 us
  matrix products: 49.1 us -> 14.2 us
  blocking collectives: 28.3 us -> 0 us
  between operations: 14.2 us -> 0.66 us
  local copies, waits for them, and re-layouts: 12.6 us -> 1.54 us
  other arithmetic: 11 us -> 0 us
    reduce_scatter x4 -> x0, waiting for transfers between devices: 189 us -> none  [the longest x1 105 us: shards(): lax.psum_scatter(jnp.concatenate([jnp.dot(block_rows, w_gate, preferred_e...]
    pallas_call x0 -> x1, Pallas kernels: none -> 156 us  [ring_call(): pl.pallas_call(kernel, out_shape=(wide, wide, wide, model, model, jax.Sha...]
    all_gather x3 -> x0, waiting for transfers between devices: 140 us -> none  [the longest x1 47.9 us: shards(): lax.all_gather(gate_grad, 'col', axis=0, tiled=True)]
    dot_general x6 -> x0, matrix products: 31.1 us -> none  [the longest x3 18.6 us: matmul_nt(): lax.dot_general(left, right, (((1,), (1,)), ((), ())), preferred_element_...]
    all_gather x2 -> x0, blocking collectives: 28.3 us -> none  [the longest x1 15.2 us: shards(): cotan_all = lax.all_gather(cotangent, 'row', axis=0, tiled=True)]
    unnamed x6 -> x8, local copies, waits for them, and re-layouts: 12.6 us -> 0.02 us
    concatenate x1 -> x0, other arithmetic: 5.61 us -> none  [shards(): jnp.concatenate([jnp.dot(block_rows, w_gate, preferred_element_type=jnp.f...]
    convert_element_type x3 -> x0, other arithmetic: 5.42 us -> none  [the longest x1 2.34 us: shards(): up_grad = (hidden_grad * activated).astype(jnp.bfloat16)]
  transfers between devices with their start and end apart: 7 -> 0, of which waited for: 6 -> 0; matrix products, arithmetic and copies ran while one was open for 14% -> 0% of each run, Pallas kernels for 0% -> 0%
where the time goes in v1:
time: 173 us
  Pallas kernels  156 us (90%)
  matrix products  14.2 us (8%)
    pallas_call x1, Pallas kernels, ring_call(): pl.pallas_call(kernel, out_shape=(wide, wide, wide, model, model, jax.Sha...  156 us
    dot_general x3, matrix products, matmul_tn(): lax.dot_general(left, right, (((0,), (0,)), ((), ())), preferred_element_...  14.2 us

profile of v1, /device:TPU:1, one launch (start us, length us, event | category | flops | bytes accessed | tf_op | source)
XLA Modules:
  0.0 172.8 jit_solution(13982580275499268234)
XLA Ops:
  0.6 156.4 %ring_sums.1 = (bf16[4,4,32,3584]{3,2,1,0:T(8,128)(2,1)}, bf16[4,4,32,3584]{3,2,1,0:T(8,128)(2,1)}, bf16[4,4,32,3584]{3,2,1,0:T(8,128)(2,1)}, bf16[4,4,32,512]{3...) custom-call(bf16[64,512]{1,0:T(8,128)(2,1)} %refs_0_.1, bf16[64,512]{1,0:T(8,128)(2,1)} %refs_1_.1, ...), custom_call_target="tpu_custom_call" | custom-call | tf_op jit(solution)/shard_map/ring_sums/pallas_call | solution.py:394
  157.1 1.5 slice_bitcast_fusion
  158.6 0.0 copy-start
  158.6 0.0 copy-start.1
  158.6 6.3 %bitcast_convert_fusion.2 = bf16[512,3584]{1,0:T(8,128)(2,1)} fusion(bf16[4,4,32,512]{3,2,1,0:T(8,128)(2,1)} %get-tuple-element.12, bf16[4,4,32,3584]{3,2,1,0:T(8,128)(2,1)} %get-tuple-element.13), kind=kOutput, calls=%fused_computation.2 | convolution fusion | flops 1880883200 | bytes 7864320 | tf_op jit(solution)/shard_map/dot_general | solution.py:437
  164.9 0.0 copy-done
  164.9 0.0 copy-done.1
  164.9 0.0 copy-start.2
  164.9 0.0 copy-start.3
  164.9 3.9 %bitcast_convert_fusion.1 = bf16[512,3584]{1,0:T(8,128)(2,1)} fusion(bf16[4,4,32,512]{3,2,1,0:T(8,128)(2,1)S(1)} %copy-done.1, bf16[4,4,32,3584]{3,2,1,0:T(8,128)(2,1)S(1)} %copy-done), kind=kOutput, calls=%fused_computation.1 | convolution fusion | flops 1880883200 | bytes 7864320 | tf_op jit(solution)/shard_map/dot_general | solution.py:437
  168.8 0.0 copy-done.2
  168.8 0.0 copy-done.3
  168.8 3.9 %bitcast_convert_fusion = bf16[3584,512]{1,0:T(8,128)(2,1)} fusion(bf16[4,4,32,3584]{3,2,1,0:T(8,128)(2,1)S(1)} %copy-done.2, bf16[4,4,32,512]{3,2,1,0:T(8,128)(2,1)S(1)} %copy-done.3), kind=kOutput, calls=%fused_computation | convolution fusion | flops 1880883200 | bytes 7864320 | tf_op jit(solution)/shard_map/dot_general | solution.py:437
Async XLA Ops:
  158.6 6.3 %copy-start = (bf16[4,4,32,3584]{3,2,1,0:T(8,128)(2,1)S(1)}, bf16[4,4,32,3584]{3,2,1,0:T(8,128)(2,1)}, u32[]{:S(2)}) copy-start(bf16[4,4,32,3584]{3,2,1,0:T(8,128)(2,1)} %get-tuple-element.14) | copy-start | bytes 11010052
  158.6 6.3 %copy-start.1 = (bf16[4,4,32,512]{3,2,1,0:T(8,128)(2,1)S(1)}, bf16[4,4,32,512]{3,2,1,0:T(8,128)(2,1)}, u32[]{:S(2)}) copy-start(bf16[4,4,32,512]{3,2,1,0:T(8,128)(2,1)} %get-tuple-element.12) | copy-start | bytes 1572868
  164.9 4.0 %copy-start.2 = (bf16[4,4,32,3584]{3,2,1,0:T(8,128)(2,1)S(1)}, bf16[4,4,32,3584]{3,2,1,0:T(8,128)(2,1)}, u32[]{:S(2)}) copy-start(bf16[4,4,32,3584]{3,2,1,0:T(8,128)(2,1)} %get-tuple-element.15) | copy-start | bytes 11010052
  164.9 4.0 %copy-start.3 = (bf16[4,4,32,512]{3,2,1,0:T(8,128)(2,1)S(1)}, bf16[4,4,32,512]{3,2,1,0:T(8,128)(2,1)}, u32[]{:S(2)}) copy-start(bf16[4,4,32,512]{3,2,1,0:T(8,128)(2,1)} %get-tuple-element.16) | copy-start | bytes 1572868

commit v2 on v1

--- a/solution.py
+++ b/solution.py
@@ -10,6 +10,9 @@
 F32 = jnp.float32
 WIDTH = 256
 DEPTH = 8
+EARLY = 4
+AHEAD = 2
+KEEP_PARTS = 2
 
 FAR_UP, FAR_DOWN, OWN_UP, OWN_DOWN, SUM_UP, SUM_DOWN = range(6)
 SECOND = 6
@@ -26,14 +29,19 @@
     return lax.dot_general(left, right, (((1,), (1,)), ((), ())), preferred_element_type=F32)
 
 
+def dot_tn(left, right):
+    return lax.dot_general(left, right, (((0,), (0,)), ((), ())), preferred_element_type=F32)
+
+
 def ring_kernel(
     steps,
     tok_ref, cot_ref, wg_hbm, wu_hbm, wd_hbm,
-    hid_out, gg_out, ug_out, tok_out, cot_out, mi_out,
+    gg_out, ug_out, dg_out, own_out, sum1, sum2, sum3,
     wg, wu, wd, nat, perm, far, far_in, near, near_in,
-    far2, far2_in, near2, near2_in, sub, all3, acc, core_in, y_send, y_in,
-    send_sem, recv_sem, w_sem, out_sem, g_send, g_recv, r_send, r_recv, tok_sem,
+    far2, far2_in, near2, near2_in, sub, all3, tok_t, grads, down_grads, acc, core_in, y_send, y_in,
+    send_sem, recv_sem, w_sem, out_sem, g_send, g_recv, r_send, r_recv, y_sem, tok_sem,
 ):
+    sum_outs = (own_out, sum1, sum2, sum3)
     row, col = lax.axis_index("row"), lax.axis_index("col")
     x, z, y, core = col // 4, col % 4, row // 2, row % 2
     width = WIDTH
@@ -56,9 +64,13 @@
         pltpu.make_async_copy(wg_hbm.at[:, cols], wg.at[k], w_sem.at[k, 0]).start()
         pltpu.make_async_copy(wu_hbm.at[:, cols], wu.at[k], w_sem.at[k, 1]).start()
 
-    for half in range(2):
-        nat[0, y, 2 * core + half] = tok_ref[32 * half : 32 * half + 32, :]
-        nat[1, y, 2 * core + half] = cot_ref[32 * half : 32 * half + 32, :]
+    own = [
+        pltpu.make_async_copy(ref.at[pl.ds(32 * half, 32)], nat.at[a, y, 2 * core + half], tok_sem.at[2 * a + half])
+        for a, ref in enumerate((tok_ref, cot_ref))
+        for half in range(2)
+    ]
+    for copy in own:
+        copy.start()
 
     barrier = pltpu.get_barrier_semaphore()
     peers = [at_x(x + 1), at_x(x + 3), at_z(z + 1), at_z(z + 3), at_y(y + 1), at_y(y + 2), at_y(y + 3), sibling]
@@ -66,53 +78,43 @@
         pl.semaphore_signal(barrier, inc=1, device_id=peer, device_id_type=MESH)
     pl.semaphore_wait(barrier, len(peers))
 
-    def rows_of(y_at, core_at):
-        return nat.at[:, y_at, pl.ds(2 * core_at, 2)]
-
-    def y_copy(step):
+    for copy in own:
+        copy.wait()
+
+    def rows_of(a, y_at, core_at):
+        return nat.at[a, y_at, pl.ds(2 * core_at, 2)]
+
+    def y_copy(a, step, back):
+        block = rows_of(a, lax.rem(y + back, 4), core)
         return pltpu.make_async_remote_copy(
-            src_ref=rows_of(y, core), dst_ref=rows_of(y, core), send_sem=g_send.at[step], recv_sem=g_recv.at[step],
+            src_ref=block, dst_ref=block, send_sem=g_send.at[a, step], recv_sem=g_recv.at[a, step],
             device_id=at_y(y + step), device_id_type=MESH,
         )
 
-    def y_arrival(step):
-        came = lax.rem(y + 4 - step, 4)
+    def core_copy(a, step, core_at):
+        block = rows_of(a, lax.rem(y + 4 - step, 4), core_at)
         return pltpu.make_async_remote_copy(
-            src_ref=rows_of(came, core), dst_ref=rows_of(came, core), send_sem=g_send.at[step],
-            recv_sem=g_recv.at[step], device_id=at_y(y + step), device_id_type=MESH,
+            src_ref=block, dst_ref=block, send_sem=g_send.at[a, 4 + step], recv_sem=g_recv.at[a, 4 + step],
+            device_id=sibling, device_id_type=MESH,
         )
 
-    def core_copy(step, core_at):
-        came = lax.rem(y + 4 - step, 4)
-        return pltpu.make_async_remote_copy(
-            src_ref=rows_of(came, core_at), dst_ref=rows_of(came, core_at), send_sem=g_send.at[4 + step],
-            recv_sem=g_recv.at[4 + step], device_id=sibling, device_id_type=MESH,
-        )
-
-    for step in (2, 1, 3):
-        y_copy(step).start()
-    core_copy(0, core).start()
-    for step in (1, 3, 2):
-        y_arrival(step).wait_recv()
-        core_copy(step, core).start()
-    for step in range(4):
-        core_copy(step, 1 - core).wait_recv()
-    for step in (1, 2, 3):
-        y_copy(step).wait_send()
-    for step in range(4):
-        core_copy(step, core).wait_send()
-
-    for i in range(4):
-        for j in range(4):
-            perm[:, j, i] = nat[:, i, j]
-    keep = (
-        pltpu.make_async_copy(nat.at[0], tok_out, tok_sem.at[0]),
-        pltpu.make_async_copy(nat.at[1], cot_out, tok_sem.at[1]),
-    )
-    for copy in keep:
-        copy.start()
+    def gathered(a):
+        for step in (0, 1, 3, 2):
+            core_copy(a, step, 1 - core).wait_recv()
+        for i in range(4):
+            for j in range(4):
+                perm[a, j, i] = nat[a, i, j]
+
+    for a in (1, 0):
+        for step in (1, 3, 2):
+            y_copy(a, step, 0).start()
+        core_copy(a, 0, core).start()
     acc[...] = jnp.zeros_like(acc)
-
+    for a in (1, 0):
+        for step in (1, 3, 2):
+            y_copy(a, step, 4 - step).wait_recv()
+            core_copy(a, step, core).start()
+    gathered(1)
     def part(h, k, a, block, first, count):
         tokens = (nat, perm)[h]
         left = tokens[1 if a == 2 else 0, block, pl.ds(first, count)].reshape(count * 32, -1)
@@ -166,10 +168,12 @@
         held(WIDE_PASS_DOWN, all3.at[at, :, p_up, high], all3.at[at, :, opp_p, high], down)
         return table
 
-    def start(k, h, *kinds):
+    def start(k, h, *kinds, arrays=None):
         table = copies(k, h)
         for kind in kinds:
             src, dst, target, _ = table[kind]
+            if arrays is not None:
+                src, dst = src.at[arrays], dst.at[arrays]
             copy_of(kind, k, h, src, dst, target).start()
 
     def arrive(k, h, *kinds):
@@ -182,23 +186,56 @@
         for kind, (src, dst, target, _) in copies(k, h).items():
             copy_of(kind, k, h, src, dst, target).wait_send()
 
+    def first_sums(k, h, a):
+        p = rings[h][0]
+        at = 2 * k + h
+        whole = part(h, k, a, lax.rem(p + 2, 4), 0, 4).astype(BF16)
+        far[at, 0, a] = whole[:64]
+        far[at, 1, a] = whole[64:]
+        near[at, 0, 1, a] = part(h, k, a, lax.rem(p + 1, 4), 2, 2).astype(BF16)
+        near[at, 1, 0, a] = part(h, k, a, lax.rem(p + 3, 4), 0, 2).astype(BF16)
+
+    firsts = (FAR_UP, FAR_DOWN, OWN_UP, OWN_DOWN)
+
+    def hidden_grad_sums(k):
+        cols = pl.ds(0, 2 * width)
+        pltpu.make_async_copy(wd_hbm.at[cols, :], wd.at[k], w_sem.at[k, 2]).wait()
+        for h in range(2):
+            first_sums(k, h, 2)
+
     def stage0(k):
         cols = pl.ds(0, 2 * width)
-        pltpu.make_async_copy(wd_hbm.at[cols, :], wd.at[k], w_sem.at[k, 2]).wait()
+
+        @pl.when(k == 0)
+        def _():
+            for ahead in range(AHEAD):
+                hidden_grad_sums(ahead)
+                for h in range(2):
+                    start(ahead, h, *firsts, arrays=pl.ds(2, 1))
+            gathered(0)
+
+        @pl.when(k >= AHEAD)
+        def _():
+            hidden_grad_sums(k)
+
         pltpu.make_async_copy(wg_hbm.at[:, cols], wg.at[k], w_sem.at[k, 0]).wait()
         pltpu.make_async_copy(wu_hbm.at[:, cols], wu.at[k], w_sem.at[k, 1]).wait()
         for h in range(2):
-            p = rings[h][0]
-            at = 2 * k + h
-            for a in range(3):
-                whole = part(h, k, a, lax.rem(p + 2, 4), 0, 4).astype(BF16)
-                far[at, 0, a] = whole[:64]
-                far[at, 1, a] = whole[64:]
-            start(k, h, FAR_UP, FAR_DOWN)
-            for a in range(3):
-                near[at, 0, 1, a] = part(h, k, a, lax.rem(p + 1, 4), 2, 2).astype(BF16)
-                near[at, 1, 0, a] = part(h, k, a, lax.rem(p + 3, 4), 0, 2).astype(BF16)
-            start(k, h, OWN_UP, OWN_DOWN)
+            for a in range(2):
+                first_sums(k, h, a)
+
+            @pl.when(k < AHEAD)
+            def _():
+                start(k, h, *firsts, arrays=pl.ds(0, 2))
+
+            @pl.when(k >= AHEAD)
+            def _():
+                start(k, h, *firsts)
+
+        @pl.when(k == 0)
+        def _():
+            for h, tokens in enumerate((nat, perm)):
+                tok_t[h] = tokens[0].reshape(tok_t.shape[1:]).T
 
     def stage1(k):
         for h in range(2):
@@ -290,24 +327,39 @@
             arrive(k, h, WIDE_UP, WIDE_DOWN)
             start(k, h, WIDE_PASS_UP, WIDE_PASS_DOWN)
 
-    def keeps(k):
+    def grad_copies(k):
+        slot = lax.rem(k, 2)
         copies_out = []
         for h in range(2):
+            span = pl.ds(pl.multiple_of((2 * k + h) * width, width), width)
+            for a, (out, src) in enumerate(
+                ((gg_out.at[:, span], grads.at[slot, h, 0]), (ug_out.at[:, span], grads.at[slot, h, 1]),
+                 (dg_out.at[span, :], down_grads.at[slot, h]))
+            ):
+                copies_out.append(pltpu.make_async_copy(src, out, out_sem.at[k, h, a]))
+        return copies_out
+
+    def stage9(k):
+        slot = lax.rem(k, 2)
+
+        @pl.when(k >= 2)
+        def _():
+            for copy in grad_copies(k - 2):
+                copy.wait()
+
+        for h in range(2):
             at = 2 * k + h
-            cols = pl.ds(pl.multiple_of(at * width, width), width)
-            for a, out in enumerate((hid_out, gg_out, ug_out)):
-                if h == 0:
-                    copies_out.append((all3.at[at, a], out.at[:, :, :, cols], 5 * a))
-                else:
-                    for j in range(4):
-                        copies_out.append((all3.at[at, a, j], out.at[:, j, :, cols], 5 * a + 1 + j))
-        return [pltpu.make_async_copy(src, dst, out_sem.at[k, n]) for src, dst, n in copies_out]
+            for a in range(2):
+                grads[slot, h, a] = dot(tok_t[h], all3[at, 1 + a].reshape(512, width)).astype(BF16)
+            cot_all = (nat, perm)[h][1].reshape(512, -1)
+            down_grads[slot, h] = dot_tn(all3[at, 0].reshape(512, width), cot_all).astype(BF16)
+        for copy in grad_copies(k):
+            copy.start()
 
     def stage8(k):
+        late = (k >= EARLY).astype(jnp.int32)
         for h in range(2):
             arrive(k, h, WIDE_PASS_UP, WIDE_PASS_DOWN)
-        for copy in keeps(k):
-            copy.start()
         for h in range(2):
             at = 2 * k + h
             sent(k, h)
@@ -319,63 +371,81 @@
                 for j in range(4):
                     rows = slice(32 * j, 32 * j + 32)
                     i, jj = (b, j) if h == 0 else (j, b)
-                    acc[0, i, jj] += mixed[rows]
-                    acc[1, i, jj] += into[rows]
-
-    stages = (stage0, stage1, stage2, stage3, stage4, stage5, stage6, stage7, stage8)
+                    acc[late, 0, i, jj] += mixed[rows]
+                    acc[late, 1, i, jj] += into[rows]
+
+    order = (2, 1, 3, 0)
+
+    def core_sum(late, step):
+        block = acc.at[late, :, lax.rem(y + step, 4), pl.ds(2 * (1 - core), 2)]
+        return pltpu.make_async_remote_copy(
+            src_ref=block, dst_ref=core_in.at[late, step], send_sem=r_send.at[late, step],
+            recv_sem=r_recv.at[late, step], device_id=sibling, device_id_type=MESH,
+        )
+
+    def chip_sum(late, step):
+        core_sum(late, step).wait_recv()
+        return acc[late, :, lax.rem(y + step, 4), pl.ds(2 * core, 2)] + core_in[late, step]
+
+    def y_sum(step):
+        return pltpu.make_async_remote_copy(
+            src_ref=y_send.at[step], dst_ref=y_in.at[step], send_sem=y_sem.at[0, step], recv_sem=y_sem.at[1, step],
+            device_id=at_y(y + step), device_id_type=MESH,
+        )
+
+    stages = (stage0, stage1, stage2, stage3, stage4, stage5, stage6, stage7, stage8, stage9)
 
     def turn(i, carry):
         for late, stage in enumerate(stages):
             @pl.when((i >= late) & (i < steps + late))
             def _():
                 stage(i - late)
+
+            if late == 8:
+                @pl.when(i == EARLY + DEPTH - 1)
+                def _():
+                    for step in order:
+                        core_sum(0, step).start()
+
+            if late == 9:
+                @pl.when(i == EARLY + DEPTH - 1)
+                def _():
+                    for step in order:
+                        y_send[step] = chip_sum(0, step)
+                        if step:
+                            y_sum(step).start()
+
         return carry
 
     lax.fori_loop(0, steps + DEPTH, turn, 0)
 
-    def acc_rows(y_at, core_at):
-        return acc.at[:, y_at, pl.ds(2 * core_at, 2)]
-
-    def core_sum(step):
-        return pltpu.make_async_remote_copy(
-            src_ref=acc_rows(lax.rem(y + step, 4), 1 - core), dst_ref=core_in.at[step], send_sem=r_send.at[step],
-            recv_sem=r_recv.at[step], device_id=sibling, device_id_type=MESH,
-        )
-
-    def y_sum(step):
-        return pltpu.make_async_remote_copy(
-            src_ref=y_send.at[step], dst_ref=y_in.at[step], send_sem=r_send.at[4 + step],
-            recv_sem=r_recv.at[4 + step], device_id=at_y(y + step), device_id_type=MESH,
-        )
-
-    order = (2, 1, 3, 0)
     for step in order:
-        core_sum(step).start()
-    for step in order:
-        core_sum(step).wait_recv()
-        total = acc[:, lax.rem(y + step, 4), pl.ds(2 * core, 2)] + core_in[step]
-        y_send[step] = total
-        if step:
-            y_sum(step).start()
+        core_sum(1, step).start()
+    stage9(steps - 1)
+    for step in order[:3]:
+        total = chip_sum(1, step)
+        for j in range(2):
+            sum_outs[step][:, 32 * j : 32 * j + 32, :] = total[:, j].astype(BF16)
+    total = chip_sum(1, 0) + y_send[0]
     for step in (1, 3, 2):
         y_sum(step).wait_recv()
-    result = y_send[0] + y_in[1] + y_in[2] + y_in[3]
+        total += y_in[step]
     for j in range(2):
-        mi_out[:, 32 * j : 32 * j + 32, :] = result[:, j].astype(BF16)
+        own_out[:, 32 * j : 32 * j + 32, :] = total[:, j]
     for step in order:
-        core_sum(step).wait_send()
+        for late in range(2):
+            core_sum(late, step).wait_send()
         if step:
             y_sum(step).wait_send()
-
-    for copy in keep:
-        copy.wait()
-
-    def finish(k, carry):
-        for copy in keeps(k):
+    for a in range(2):
+        for step in (1, 2, 3):
+            y_copy(a, step, 0).wait_send()
+        for step in range(4):
+            core_copy(a, step, core).wait_send()
+
+    for k in (steps - 2, steps - 1):
+        for copy in grad_copies(k):
             copy.wait()
-        return carry
-
-    lax.fori_loop(0, steps, finish, 0)
 
 
 def ring_call(tokens, w_gate, w_up, w_down, cotangent):
@@ -388,14 +458,15 @@
     def kernel(*refs):
         ring_kernel(steps, *refs)
 
-    wide = jax.ShapeDtypeStruct((4, 4, 32, hidden), BF16)
-    model = jax.ShapeDtypeStruct((4, 4, 32, features), BF16)
+    wide = jax.ShapeDtypeStruct((features, hidden), BF16)
+    tall = jax.ShapeDtypeStruct((hidden, features), BF16)
     dma = pltpu.SemaphoreType.DMA
     return pl.pallas_call(
         kernel,
-        out_shape=(wide, wide, wide, model, model, jax.ShapeDtypeStruct((2, 64, features), BF16)),
-        in_specs=[vmem, vmem, any_space, any_space, any_space],
-        out_specs=(any_space,) * 5 + (vmem,),
+        out_shape=(wide, wide, tall) + (jax.ShapeDtypeStruct((2, 64, features), F32),)
+        + (jax.ShapeDtypeStruct((2, 64, features), BF16),) * 3,
+        in_specs=[any_space] * 5,
+        out_specs=(any_space,) * 3 + (vmem,) * 4,
         scratch_shapes=[
             pltpu.VMEM((steps, features, 2 * WIDTH), BF16),
             pltpu.VMEM((steps, features, 2 * WIDTH), BF16),
@@ -412,19 +483,23 @@
             pltpu.VMEM((parts, 2, 2, 3, 16, WIDTH), BF16),
             pltpu.VMEM((3, 2, 3, 4, 32, WIDTH), F32),
             pltpu.VMEM((parts, 3, 4, 4, 32, WIDTH), BF16),
-            pltpu.VMEM((2, 4, 4, 32, features), F32),
-            pltpu.VMEM((4, 2, 2, 32, features), F32),
+            pltpu.VMEM((2, features, 512), BF16),
+            pltpu.VMEM((2, 2, 2, features, WIDTH), BF16),
+            pltpu.VMEM((2, 2, WIDTH, features), BF16),
+            pltpu.VMEM((2, 2, 4, 4, 32, features), F32),
+            pltpu.VMEM((2, 4, 2, 2, 32, features), F32),
             pltpu.VMEM((4, 2, 2, 32, features), F32),
             pltpu.VMEM((4, 2, 2, 32, features), F32),
             dma((parts, COPIES)),
             dma((parts, COPIES)),
             dma((steps, 3)),
-            dma((steps, 15)),
-            dma((8,)),
-            dma((8,)),
-            dma((8,)),
-            dma((8,)),
-            dma((2,)),
+            dma((steps, 2, 3)),
+            dma((2, 8)),
+            dma((2, 8)),
+            dma((2, 4)),
+            dma((2, 4)),
+            dma((2, 4)),
+            dma((4,)),
         ],
         name="ring_sums",
         compiler_params=pltpu.CompilerParams(
@@ -433,22 +508,39 @@
     )(tokens, cotangent, w_gate, w_up, w_down)
 
 
-def matmul_tn(left, right):
-    return lax.dot_general(left, right, (((0,), (0,)), ((), ())), preferred_element_type=F32).astype(BF16)
+def along_y(block, step):
+    rows = lax.axis_size("row")
+    return lax.ppermute(block, "row", [(r, (r + 2 * step) % rows) for r in range(rows)])
+
+
+def keep_kernel(*refs):
+    for src, dst in zip(refs[:3], refs[3:]):
+        dst[...] = src[...]
+
+
+def keep(*arrays):
+    specs = [pl.BlockSpec((a.shape[0] // KEEP_PARTS, a.shape[1]), lambda i: (i, 0)) for a in arrays]
+    return pl.pallas_call(
+        keep_kernel,
+        out_shape=tuple(jax.ShapeDtypeStruct(a.shape, a.dtype) for a in arrays),
+        grid=(KEEP_PARTS,),
+        in_specs=specs,
+        out_specs=tuple(specs),
+        name="keep",
+        compiler_params=pltpu.CompilerParams(vmem_limit_bytes=62 * 2**20),
+        cost_estimate=pl.CostEstimate(flops=0, transcendentals=0, bytes_accessed=sum(4 * a.size for a in arrays)),
+    )(*arrays)
 
 
 def shards(tokens, w_gate, w_up, w_down, cotangent):
-    hidden, gate_grad, up_grad, tok_all, cot_all, sums = ring_call(tokens, w_gate, w_up, w_down, cotangent)
-    hidden, gate_grad, up_grad, tok_all, cot_all = (
-        a.reshape(512, a.shape[-1]) for a in (hidden, gate_grad, up_grad, tok_all, cot_all)
+    gate_wgrad, up_wgrad, down_wgrad, own, *sums = ring_call(tokens, w_gate, w_up, w_down, cotangent)
+    came = [along_y(block, step + 1) for step, block in enumerate(sums)]
+    weight_grads = keep(gate_wgrad, up_wgrad, down_wgrad)
+    mixed, input_grad = (
+        (own[i] + came[0][i].astype(F32) + came[1][i].astype(F32) + came[2][i].astype(F32)).astype(BF16)
+        for i in range(2)
     )
-    return (
-        sums[0],
-        sums[1],
-        matmul_tn(tok_all, gate_grad),
-        matmul_tn(tok_all, up_grad),
-        matmul_tn(hidden, cot_all),
-    )
+    return (mixed, input_grad, *weight_grads)
 
 
 def solution(mesh):

time: 173 us -> 157 us (0.908)
  matrix products: 14.2 us -> 0 us
  Pallas kernels: 156 us -> 153 us
  starting transfers between devices: 0 us -> 2.75 us
    dot_general x3 -> x0, matrix products: 14.2 us -> none  [matmul_tn(): lax.dot_general(left, right, (((0,), (0,)), ((), ())), preferred_element_...]
    pallas_call x1 -> x2, Pallas kernels: 156 us -> 153 us  [the longest x1 145 us: ring_call(): pl.pallas_call(kernel, out_shape=(wide, wide, tall) + (jax.ShapeDtypeStru...]
    ppermute x0 -> x3, starting transfers between devices: none -> 2.75 us  [along_y(): lax.ppermute(block, 'row', [(r, (r + 2 * step) % rows) for r in range(row...]
  transfers between devices with their start and end apart: 0 -> 3, of which waited for: 0 -> 0; matrix products, arithmetic and copies ran while one was open for 0% -> 0% of each run, Pallas kernels for 0% -> 5%
where the time goes in v2:
time: 157 us
  Pallas kernels  153 us (97%)
  starting transfers between devices  2.75 us (2%)
    pallas_call x1, Pallas kernels, ring_call(): pl.pallas_call(kernel, out_shape=(wide, wide, tall) + (jax.ShapeDtypeStru...  145 us
    pallas_call x1, Pallas kernels, keep(): pl.pallas_call(keep_kernel, out_shape=tuple((jax.ShapeDtypeStruct(a.shape...  7.51 us
  transfers between devices with their start and end apart: 3, of which 0 were waited for; matrix products, arithmetic and copies ran while one was open for 0% of the time, Pallas kernels for 5%

profile of v2, /device:TPU:1, one launch (start us, length us, event | category | flops | bytes accessed | tf_op | source)
XLA Modules:
  0.0 156.9 jit_solution(4267758433002668359)
XLA Ops:
  0.6 145.2 %ring_sums.1 = (bf16[512,3584]{1,0:T(8,128)(2,1)}, bf16[512,3584]{1,0:T(8,128)(2,1)}, bf16[3584,512]{1,0:T(8,128)(2,1)}, f32[2,64,512]{2,1,0:T(8,128)}, bf16[2,6...) custom-call(bf16[64,512]{1,0:T(8,128)(2,1)} %refs_0_.1, bf16[64,512]{1,0:T(8,128)(2,1)} %refs_1_.1, ...), custom_call_target="tpu_custom_call" | custom-call | tf_op jit(solution)/shard_map/ring_sums/pallas_call | solution.py:464
  145.8 0.2 collective-permute-start
  146.0 1.8 %collective-permute-start.1 = (bf16[2,64,512]{2,1,0:T(8,128)(2,1)}, bf16[2,64,512]{2,1,0:T(8,128)(2,1)S(1)}, u32[]{:S(2)}, u32[]{:S(2)}) collective-permute-start(bf16[2,64,512]{2,1,0:T(8,128)(2,1)} %get-tuple-element.17), channel_id=1, source_target_pairs={{0,64},{16,80},{32,96},{48,112},{64,0},{80,16},{96,32},{112,48},{1... | collective-permute-start | bytes 393224 | tf_op jit(solution)/shard_map/ppermute | solution.py:513
  147.8 0.7 collective-permute-start.2
  148.6 0.0 copy-start
  148.6 7.5 %keep.1 = (bf16[512,3584]{1,0:T(8,128)(2,1)}, bf16[512,3584]{1,0:T(8,128)(2,1)}, bf16[3584,512]{1,0:T(8,128)(2,1)}) custom-call(bf16[512,3584]{1,0:T(8,128)(2,1)} %get-tuple-element.19.refs_0_, bf16[512,3584]{1,0:T(8,128)(2,1)} %get-tuple-element.20.refs_1_, bf16[3584,512]{1,0:T(8,128)(2,1)} %get-tuple-element.21.refs_2_), custom_call_target="tpu_custom_call" | custom-call | bytes 22020096 | tf_op jit(solution)/shard_map/keep/pallas_call | solution.py:523
  156.1 0.0 collective-permute-done
  156.1 0.0 collective-permute-done.1
  156.1 0.0 collective-permute-done.2
  156.1 0.0 copy-done
  156.1 0.7 fusion.1
Async XLA Ops:
  145.8 10.3 %collective-permute-start = (bf16[2,64,512]{2,1,0:T(8,128)(2,1)}, bf16[2,64,512]{2,1,0:T(8,128)(2,1)S(1)}, u32[]{:S(2)}, u32[]{:S(2)}) collective-permute-start(bf16[2,64,512]{2,1,0:T(8,128)(2,1)} %get-tuple-element.16), channel_id=1, source_target_pairs={{0,32},{16,48},{32,64},{48,80},{64,96},{80,112},{96,0},{112,16},{1... | collective-permute-start | bytes 393224 | tf_op jit(solution)/shard_map/ppermute | solution.py:513
  146.0 10.1 %collective-permute-start.1 = (bf16[2,64,512]{2,1,0:T(8,128)(2,1)}, bf16[2,64,512]{2,1,0:T(8,128)(2,1)S(1)}, u32[]{:S(2)}, u32[]{:S(2)}) collective-permute-start(bf16[2,64,512]{2,1,0:T(8,128)(2,1)} %get-tuple-element.17), channel_id=1, source_target_pairs={{0,64},{16,80},{32,96},{48,112},{64,0},{80,16},{96,32},{112,48},{1... | collective-permute-start | bytes 393224 | tf_op jit(solution)/shard_map/ppermute | solution.py:513
  147.8 8.3 %collective-permute-start.2 = (bf16[2,64,512]{2,1,0:T(8,128)(2,1)}, bf16[2,64,512]{2,1,0:T(8,128)(2,1)S(1)}, u32[]{:S(2)}, u32[]{:S(2)}) collective-permute-start(bf16[2,64,512]{2,1,0:T(8,128)(2,1)} %get-tuple-element.18), channel_id=1, source_target_pairs={{0,96},{16,112},{32,0},{48,16},{64,32},{80,48},{96,64},{112,80},{1... | collective-permute-start | bytes 393224 | tf_op jit(solution)/shard_map/ppermute | solution.py:513
  148.6 7.5 %copy-start = (f32[2,64,512]{2,1,0:T(8,128)S(1)}, f32[2,64,512]{2,1,0:T(8,128)}, u32[]{:S(2)}) copy-start(f32[2,64,512]{2,1,0:T(8,128)} %get-tuple-element.15) | copy-start | bytes 786436

commit v3 on v2

--- a/solution.py
+++ b/solution.py
@@ -58,12 +58,6 @@
     sibling = (row + 1 - 2 * core, col)
     rings = ((x, z, at_x, at_z), (z, x, at_z, at_x))
 
-    for k in range(steps):
-        cols = pl.ds(k * 2 * width, 2 * width)
-        pltpu.make_async_copy(wd_hbm.at[cols, :], wd.at[k], w_sem.at[k, 2]).start()
-        pltpu.make_async_copy(wg_hbm.at[:, cols], wg.at[k], w_sem.at[k, 0]).start()
-        pltpu.make_async_copy(wu_hbm.at[:, cols], wu.at[k], w_sem.at[k, 1]).start()
-
     own = [
         pltpu.make_async_copy(ref.at[pl.ds(32 * half, 32)], nat.at[a, y, 2 * core + half], tok_sem.at[2 * a + half])
         for a, ref in enumerate((tok_ref, cot_ref))
@@ -76,6 +70,14 @@
     peers = [at_x(x + 1), at_x(x + 3), at_z(z + 1), at_z(z + 3), at_y(y + 1), at_y(y + 2), at_y(y + 3), sibling]
     for peer in peers:
         pl.semaphore_signal(barrier, inc=1, device_id=peer, device_id_type=MESH)
+    def fetch(k):
+        cols = pl.ds(k * 2 * width, 2 * width)
+        pltpu.make_async_copy(wd_hbm.at[cols, :], wd.at[k], w_sem.at[k, 2]).start()
+        pltpu.make_async_copy(wg_hbm.at[:, cols], wg.at[k], w_sem.at[k, 0]).start()
+        pltpu.make_async_copy(wu_hbm.at[:, cols], wu.at[k], w_sem.at[k, 1]).start()
+
+    fetch(0)
+    acc[...] = jnp.zeros_like(acc)
     pl.semaphore_wait(barrier, len(peers))
 
     for copy in own:
@@ -109,11 +111,15 @@
         for step in (1, 3, 2):
             y_copy(a, step, 0).start()
         core_copy(a, 0, core).start()
-    acc[...] = jnp.zeros_like(acc)
-    for a in (1, 0):
+    for k in range(1, steps):
+        fetch(k)
+
+    def along_core(a):
         for step in (1, 3, 2):
             y_copy(a, step, 4 - step).wait_recv()
             core_copy(a, step, core).start()
+
+    along_core(1)
     gathered(1)
     def part(h, k, a, block, first, count):
         tokens = (nat, perm)[h]
@@ -197,11 +203,13 @@
 
     firsts = (FAR_UP, FAR_DOWN, OWN_UP, OWN_DOWN)
 
-    def hidden_grad_sums(k):
+    def hidden_grad_sums(k, send):
         cols = pl.ds(0, 2 * width)
         pltpu.make_async_copy(wd_hbm.at[cols, :], wd.at[k], w_sem.at[k, 2]).wait()
         for h in range(2):
             first_sums(k, h, 2)
+            if send:
+                start(k, h, *firsts, arrays=pl.ds(2, 1))
 
     def stage0(k):
         cols = pl.ds(0, 2 * width)
@@ -209,14 +217,14 @@
         @pl.when(k == 0)
         def _():
             for ahead in range(AHEAD):
-                hidden_grad_sums(ahead)
-                for h in range(2):
-                    start(ahead, h, *firsts, arrays=pl.ds(2, 1))
+                hidden_grad_sums(ahead, True)
+                if ahead == 0:
+                    along_core(0)
             gathered(0)
 
         @pl.when(k >= AHEAD)
         def _():
-            hidden_grad_sums(k)
+            hidden_grad_sums(k, False)
 
         pltpu.make_async_copy(wg_hbm.at[:, cols], wg.at[k], w_sem.at[k, 0]).wait()
         pltpu.make_async_copy(wu_hbm.at[:, cols], wu.at[k], w_sem.at[k, 1]).wait()
@@ -232,7 +240,7 @@
             def _():
                 start(k, h, *firsts)
 
-        @pl.when(k == 0)
+        @pl.when(k == 3)
         def _():
             for h, tokens in enumerate((nat, perm)):
                 tok_t[h] = tokens[0].reshape(tok_t.shape[1:]).T
@@ -349,6 +357,7 @@
 
         for h in range(2):
             at = 2 * k + h
+            sent(k, h)
             for a in range(2):
                 grads[slot, h, a] = dot(tok_t[h], all3[at, 1 + a].reshape(512, width)).astype(BF16)
             cot_all = (nat, perm)[h][1].reshape(512, -1)
@@ -358,21 +367,22 @@
 
     def stage8(k):
         late = (k >= EARLY).astype(jnp.int32)
-        for h in range(2):
-            arrive(k, h, WIDE_PASS_UP, WIDE_PASS_DOWN)
-        for h in range(2):
-            at = 2 * k + h
-            sent(k, h)
-            hidden_rows = slice(h * width, (h + 1) * width)
-            for b in range(4):
-                hidden, gate_grad, up_grad = (all3[at, a, b].reshape(128, width) for a in range(3))
-                mixed = dot(hidden, wd[k, hidden_rows, :])
-                into = dot_nt(gate_grad, wg[k, :, hidden_rows]) + dot_nt(up_grad, wu[k, :, hidden_rows])
-                for j in range(4):
-                    rows = slice(32 * j, 32 * j + 32)
-                    i, jj = (b, j) if h == 0 else (j, b)
-                    acc[late, 0, i, jj] += mixed[rows]
-                    acc[late, 1, i, jj] += into[rows]
+        for last in range(2):
+            for h in range(2):
+                at = 2 * k + h
+                if last:
+                    arrive(k, h, WIDE_PASS_UP, WIDE_PASS_DOWN)
+                hidden_rows = slice(h * width, (h + 1) * width)
+                for ahead in (2,) if last else (0, 1, 3):
+                    b = lax.rem(rings[h][0] + ahead, 4)
+                    hidden, gate_grad, up_grad = (all3[at, a, b].reshape(128, width) for a in range(3))
+                    mixed = dot(hidden, wd[k, hidden_rows, :])
+                    into = dot_nt(gate_grad, wg[k, :, hidden_rows]) + dot_nt(up_grad, wu[k, :, hidden_rows])
+                    for j in range(4):
+                        rows = slice(32 * j, 32 * j + 32)
+                        i, jj = (b, j) if h == 0 else (j, b)
+                        acc[late, 0, i, jj] += mixed[rows]
+                        acc[late, 1, i, jj] += into[rows]
 
     order = (2, 1, 3, 0)
 
@@ -393,7 +403,7 @@
             device_id=at_y(y + step), device_id_type=MESH,
         )
 
-    stages = (stage0, stage1, stage2, stage3, stage4, stage5, stage6, stage7, stage8, stage9)
+    stages = (stage0, stage1, stage2, stage3, stage4, stage5, stage6, stage7, stage8)
 
     def turn(i, carry):
         for late, stage in enumerate(stages):
@@ -401,27 +411,30 @@
             def _():
                 stage(i - late)
 
-            if late == 8:
-                @pl.when(i == EARLY + DEPTH - 1)
-                def _():
-                    for step in order:
-                        core_sum(0, step).start()
-
-            if late == 9:
-                @pl.when(i == EARLY + DEPTH - 1)
-                def _():
-                    for step in order:
-                        y_send[step] = chip_sum(0, step)
-                        if step:
-                            y_sum(step).start()
-
+        @pl.when(i == EARLY + DEPTH - 1)
+        def _():
+            for step in order:
+                core_sum(0, step).start()
+
+        @pl.when(i == steps + DEPTH - 1)
+        def _():
+            for step in order:
+                core_sum(1, step).start()
+
+        @pl.when(i >= DEPTH)
+        def _():
+            stage9(i - DEPTH)
+
+        @pl.when(i == EARLY + DEPTH - 1)
+        def _():
+            for step in order:
+                y_send[step] = chip_sum(0, step)
+                if step:
+                    y_sum(step).start()
         return carry
 
     lax.fori_loop(0, steps + DEPTH, turn, 0)
 
-    for step in order:
-        core_sum(1, step).start()
-    stage9(steps - 1)
     for step in order[:3]:
         total = chip_sum(1, step)
         for j in range(2):

time: 157 us -> 152 us (0.968)
  Pallas kernels: 153 us -> 148 us
    pallas_call x1, Pallas kernels: 145 us -> 140 us  [ring_call(): pl.pallas_call(kernel, out_shape=(wide, wide, tall) + (jax.ShapeDtypeStru...]
where the time goes in v3:
time: 152 us
  Pallas kernels  148 us (97%)
  starting transfers between devices  2.9 us (2%)
    pallas_call x1, Pallas kernels, ring_call(): pl.pallas_call(kernel, out_shape=(wide, wide, tall) + (jax.ShapeDtypeStru...  140 us
    pallas_call x1, Pallas kernels, keep(): pl.pallas_call(keep_kernel, out_shape=tuple((jax.ShapeDtypeStruct(a.shape...  7.51 us
  transfers between devices with their start and end apart: 3, of which 0 were waited for; matrix products, arithmetic and copies ran while one was open for 0% of the time, Pallas kernels for 5%

profile of v3, /device:TPU:1, one launch (start us, length us, event | category | flops | bytes accessed | tf_op | source)
XLA Modules:
  0.0 152.3 jit_solution(10495644756289648111)
XLA Ops:
  0.6 140.5 %ring_sums.1 = (bf16[512,3584]{1,0:T(8,128)(2,1)}, bf16[512,3584]{1,0:T(8,128)(2,1)}, bf16[3584,512]{1,0:T(8,128)(2,1)}, f32[2,64,512]{2,1,0:T(8,128)}, bf16[2,6...) custom-call(bf16[64,512]{1,0:T(8,128)(2,1)} %refs_0_.1, bf16[64,512]{1,0:T(8,128)(2,1)} %refs_1_.1, ...), custom_call_target="tpu_custom_call" | custom-call | tf_op jit(solution)/shard_map/ring_sums/pallas_call | solution.py:477
  141.1 0.4 collective-permute-start
  141.5 1.4 collective-permute-start.1
  142.9 1.1 collective-permute-start.2
  144.0 0.0 copy-start
  144.0 7.5 %keep.1 = (bf16[512,3584]{1,0:T(8,128)(2,1)}, bf16[512,3584]{1,0:T(8,128)(2,1)}, bf16[3584,512]{1,0:T(8,128)(2,1)}) custom-call(bf16[512,3584]{1,0:T(8,128)(2,1)} %get-tuple-element.19.refs_0_, bf16[512,3584]{1,0:T(8,128)(2,1)} %get-tuple-element.20.refs_1_, bf16[3584,512]{1,0:T(8,128)(2,1)} %get-tuple-element.21.refs_2_), custom_call_target="tpu_custom_call" | custom-call | bytes 22020096 | tf_op jit(solution)/shard_map/keep/pallas_call | solution.py:536
  151.5 0.0 collective-permute-done
  151.5 0.0 collective-permute-done.1
  151.5 0.0 collective-permute-done.2
  151.6 0.0 copy-done
  151.6 0.7 fusion.1
Async XLA Ops:
  141.1 10.4 %collective-permute-start = (bf16[2,64,512]{2,1,0:T(8,128)(2,1)}, bf16[2,64,512]{2,1,0:T(8,128)(2,1)S(1)}, u32[]{:S(2)}, u32[]{:S(2)}) collective-permute-start(bf16[2,64,512]{2,1,0:T(8,128)(2,1)} %get-tuple-element.16), channel_id=1, source_target_pairs={{0,32},{16,48},{32,64},{48,80},{64,96},{80,112},{96,0},{112,16},{1... | collective-permute-start | bytes 393224 | tf_op jit(solution)/shard_map/ppermute | solution.py:526
  141.5 10.0 %collective-permute-start.1 = (bf16[2,64,512]{2,1,0:T(8,128)(2,1)}, bf16[2,64,512]{2,1,0:T(8,128)(2,1)S(1)}, u32[]{:S(2)}, u32[]{:S(2)}) collective-permute-start(bf16[2,64,512]{2,1,0:T(8,128)(2,1)} %get-tuple-element.17), channel_id=1, source_target_pairs={{0,64},{16,80},{32,96},{48,112},{64,0},{80,16},{96,32},{112,48},{1... | collective-permute-start | bytes 393224 | tf_op jit(solution)/shard_map/ppermute | solution.py:526
  142.9 8.7 %collective-permute-start.2 = (bf16[2,64,512]{2,1,0:T(8,128)(2,1)}, bf16[2,64,512]{2,1,0:T(8,128)(2,1)S(1)}, u32[]{:S(2)}, u32[]{:S(2)}) collective-permute-start(bf16[2,64,512]{2,1,0:T(8,128)(2,1)} %get-tuple-element.18), channel_id=1, source_target_pairs={{0,96},{16,112},{32,0},{48,16},{64,32},{80,48},{96,64},{112,80},{1... | collective-permute-start | bytes 393224 | tf_op jit(solution)/shard_map/ppermute | solution.py:526
  144.0 7.5 %copy-start = (f32[2,64,512]{2,1,0:T(8,128)S(1)}, f32[2,64,512]{2,1,0:T(8,128)}, u32[]{:S(2)}) copy-start(f32[2,64,512]{2,1,0:T(8,128)} %get-tuple-element.15) | copy-start | bytes 786436

commit v4 on v3

--- a/solution.py
+++ b/solution.py
@@ -18,7 +18,8 @@
 SECOND = 6
 GIVE_UP, GIVE_DOWN, PASS_UP, PASS_DOWN = range(12, 16)
 WIDE_UP, WIDE_DOWN, WIDE_PASS_UP, WIDE_PASS_DOWN = range(16, 20)
-COPIES = 20
+REST_UP, REST_DOWN = range(20, 22)
+COPIES = 22
 
 
 def dot(left, right):
@@ -167,9 +168,11 @@
         low, high = pl.ds(0, 16), pl.ds(16, 16)
         held(PASS_UP, all3.at[at, :, p, q_down, low], all3.at[at, :, p, opp_q, low], up2)
         held(PASS_DOWN, all3.at[at, :, p, q_up, high], all3.at[at, :, p, opp_q, high], down2)
-        held(WIDE_UP, all3.at[at, :, p], all3.at[at, :, p_down], up)
-        held(WIDE_DOWN, all3.at[at, :, p], all3.at[at, :, p_up], down)
         low, high = pl.ds(0, 2), pl.ds(2, 2)
+        held(WIDE_UP, all3.at[at, :, p, low], all3.at[at, :, p_down, low], up)
+        held(WIDE_DOWN, all3.at[at, :, p, high], all3.at[at, :, p_up, high], down)
+        held(REST_UP, all3.at[at, :, p, high], all3.at[at, :, p_down, high], up)
+        held(REST_DOWN, all3.at[at, :, p, low], all3.at[at, :, p_up, low], down)
         held(WIDE_PASS_UP, all3.at[at, :, p_down, low], all3.at[at, :, opp_p, low], up)
         held(WIDE_PASS_DOWN, all3.at[at, :, p_up, high], all3.at[at, :, opp_p, high], down)
         return table
@@ -332,6 +335,8 @@
 
     def stage7(k):
         for h in range(2):
+            start(k, h, REST_UP, REST_DOWN)
+        for h in range(2):
             arrive(k, h, WIDE_UP, WIDE_DOWN)
             start(k, h, WIDE_PASS_UP, WIDE_PASS_DOWN)
 
@@ -370,10 +375,12 @@
         for last in range(2):
             for h in range(2):
                 at = 2 * k + h
-                if last:
-                    arrive(k, h, WIDE_PASS_UP, WIDE_PASS_DOWN)
                 hidden_rows = slice(h * width, (h + 1) * width)
                 for ahead in (2,) if last else (0, 1, 3):
+                    if ahead == 1:
+                        arrive(k, h, REST_UP, REST_DOWN)
+                    if ahead == 2:
+                        arrive(k, h, WIDE_PASS_UP, WIDE_PASS_DOWN)
                     b = lax.rem(rings[h][0] + ahead, 4)
                     hidden, gate_grad, up_grad = (all3[at, a, b].reshape(128, width) for a in range(3))
                     mixed = dot(hidden, wd[k, hidden_rows, :])

time: 152 us -> 151 us (level)
  no operation moved by 1% of the time
where the time goes in v4:
time: 151 us
  Pallas kernels  147 us (97%)
  starting transfers between devices  2.93 us (2%)
    pallas_call x1, Pallas kernels, ring_call(): pl.pallas_call(kernel, out_shape=(wide, wide, tall) + (jax.ShapeDtypeStru...  139 us
    pallas_call x1, Pallas kernels, keep(): pl.pallas_call(keep_kernel, out_shape=tuple((jax.ShapeDtypeStruct(a.shape...  7.51 us
  transfers between devices with their start and end apart: 3, of which 0 were waited for; matrix products, arithmetic and copies ran while one was open for 0% of the time, Pallas kernels for 5%

profile of v4, /device:TPU:1, one launch (start us, length us, event | category | flops | bytes accessed | tf_op | source)
XLA Modules:
  0.0 151.1 jit_solution(10614092930559501612)
XLA Ops:
  0.6 139.2 %ring_sums.1 = (bf16[512,3584]{1,0:T(8,128)(2,1)}, bf16[512,3584]{1,0:T(8,128)(2,1)}, bf16[3584,512]{1,0:T(8,128)(2,1)}, f32[2,64,512]{2,1,0:T(8,128)}, bf16[2,6...) custom-call(bf16[64,512]{1,0:T(8,128)(2,1)} %refs_0_.1, bf16[64,512]{1,0:T(8,128)(2,1)} %refs_1_.1, ...), custom_call_target="tpu_custom_call" | custom-call | tf_op jit(solution)/shard_map/ring_sums/pallas_call | solution.py:484
  139.9 0.4 collective-permute-start
  140.3 1.6 %collective-permute-start.1 = (bf16[2,64,512]{2,1,0:T(8,128)(2,1)}, bf16[2,64,512]{2,1,0:T(8,128)(2,1)S(1)}, u32[]{:S(2)}, u32[]{:S(2)}) collective-permute-start(bf16[2,64,512]{2,1,0:T(8,128)(2,1)} %get-tuple-element.17), channel_id=1, source_target_pairs={{0,64},{16,80},{32,96},{48,112},{64,0},{80,16},{96,32},{112,48},{1... | collective-permute-start | bytes 393224 | tf_op jit(solution)/shard_map/ppermute | solution.py:533
  141.9 0.9 collective-permute-start.2
  142.8 0.0 copy-start
  142.8 7.5 %keep.1 = (bf16[512,3584]{1,0:T(8,128)(2,1)}, bf16[512,3584]{1,0:T(8,128)(2,1)}, bf16[3584,512]{1,0:T(8,128)(2,1)}) custom-call(bf16[512,3584]{1,0:T(8,128)(2,1)} %get-tuple-element.19.refs_0_, bf16[512,3584]{1,0:T(8,128)(2,1)} %get-tuple-element.20.refs_1_, bf16[3584,512]{1,0:T(8,128)(2,1)} %get-tuple-element.21.refs_2_), custom_call_target="tpu_custom_call" | custom-call | bytes 22020096 | tf_op jit(solution)/shard_map/keep/pallas_call | solution.py:543
  150.3 0.0 collective-permute-done
  150.3 0.0 collective-permute-done.1
  150.3 0.0 collective-permute-done.2
  150.3 0.0 copy-done
  150.3 0.7 fusion.1
Async XLA Ops:
  139.9 10.4 %collective-permute-start = (bf16[2,64,512]{2,1,0:T(8,128)(2,1)}, bf16[2,64,512]{2,1,0:T(8,128)(2,1)S(1)}, u32[]{:S(2)}, u32[]{:S(2)}) collective-permute-start(bf16[2,64,512]{2,1,0:T(8,128)(2,1)} %get-tuple-element.16), channel_id=1, source_target_pairs={{0,32},{16,48},{32,64},{48,80},{64,96},{80,112},{96,0},{112,16},{1... | collective-permute-start | bytes 393224 | tf_op jit(solution)/shard_map/ppermute | solution.py:533
  140.3 10.0 %collective-permute-start.1 = (bf16[2,64,512]{2,1,0:T(8,128)(2,1)}, bf16[2,64,512]{2,1,0:T(8,128)(2,1)S(1)}, u32[]{:S(2)}, u32[]{:S(2)}) collective-permute-start(bf16[2,64,512]{2,1,0:T(8,128)(2,1)} %get-tuple-element.17), channel_id=1, source_target_pairs={{0,64},{16,80},{32,96},{48,112},{64,0},{80,16},{96,32},{112,48},{1... | collective-permute-start | bytes 393224 | tf_op jit(solution)/shard_map/ppermute | solution.py:533
  141.9 8.4 %collective-permute-start.2 = (bf16[2,64,512]{2,1,0:T(8,128)(2,1)}, bf16[2,64,512]{2,1,0:T(8,128)(2,1)S(1)}, u32[]{:S(2)}, u32[]{:S(2)}) collective-permute-start(bf16[2,64,512]{2,1,0:T(8,128)(2,1)} %get-tuple-element.18), channel_id=1, source_target_pairs={{0,96},{16,112},{32,0},{48,16},{64,32},{80,48},{96,64},{112,80},{1... | collective-permute-start | bytes 393224 | tf_op jit(solution)/shard_map/ppermute | solution.py:533
  142.8 7.5 %copy-start = (f32[2,64,512]{2,1,0:T(8,128)S(1)}, f32[2,64,512]{2,1,0:T(8,128)}, u32[]{:S(2)}) copy-start(f32[2,64,512]{2,1,0:T(8,128)} %get-tuple-element.15) | copy-start | bytes 786436
